TPU v7x, 128 devices: a whole 4x4x4 slice. The times are simulated.
128 devices in a mesh: gx: 8 (over z_lo, y), gy: 8 (over x, core), gz: 2 (over z_hi).
Axes of the slice: x: 4, y: 4, z: 4 (z_hi: 2, z_lo: 2; z = z_hi * 2 + z_lo), core: 2. Of those that a mesh axis runs over, the one named last changes fastest.
Arguments:
- pressure: float32 [256, 256, 256], P('gx', 'gy', 'gz'), may hold values from -2.5 to 2.5
- source: float32 [256, 256, 256], P('gx', 'gy', 'gz'), may hold values from -40 to 40
- saturation: float32 [256, 256, 256], P('gx', 'gy', 'gz'), may hold values from 0.1 to 0.9
- permeability: float32 [256, 256, 256], P('gx', 'gy', 'gz'), may hold values from 0.1 to 10
- compress: float32 [256, 256, 256], P('gx', 'gy', 'gz'), may hold values from 0.1 to 1
- porosity: float32 [256, 256, 256], P('gx', 'gy', 'gz'), may hold values from 0.1 to 0.3
- rock_type: int32 [256, 256, 256], P('gx', 'gy', 'gz'), may hold values from 0 to 7
- well_mask: int32 [256, 256, 256], P('gx', 'gy', 'gz'), may hold values 0 or 1
- oil_factor: float32 [8], replicated, may hold values from 0.3 to 3
Outputs:
- pressure_new: float32 [256, 256, 256], P('gx', 'gy', 'gz')
- residual_new: float32 [256, 256, 256], P('gx', 'gy', 'gz')
- saturation_new: float32 [256, 256, 256], P('gx', 'gy', 'gz')
All inputs are finite; a program needn't handle non-finite values. No bound on the sum of `well_mask` on one device may be relied on, other than what follows from the above.
Results may differ from a plain program's by a relative error of at most 0.0003.
Values sent between devices are 32-bit elements; how exact they have to be, the bound alone decides.
A program may use at most 64 MiB of HBM per device.

v0:
```python
import functools
import math

import jax
import jax.numpy as jnp
import ml_dtypes
import numpy as np
from jax import lax
from jax.experimental import pallas as pl
from jax.experimental.pallas import tpu as pltpu
from jax.sharding import PartitionSpec as P

MESH = pl.DeviceIdType.MESH
F32 = jnp.float32
BF16 = jnp.bfloat16

CX, CY, CZ = 32, 32, 128
W = 8
BX, BY, BZ = CX + 2 * W, CY + 2 * W, CZ + 2 * W
HALF = BX // 2
KEPT = CX // 2
CPAD = 256
NEWTON = 3
WELL_INDEX = 4.0
INJECT_RATE = 2.0
TIME_STEP = 0.05


def sine_basis(length):
    points = np.arange(length, dtype=np.float64) + 1.0
    table = math.sqrt(2.0 / (length + 1)) * np.sin(
        np.outer(points, points) * (math.pi / (length + 1))
    )
    return table, 2.0 - 2.0 * np.cos(points * (math.pi / (length + 1)))


def halves(table):
    high = table.astype(np.float32).astype(ml_dtypes.bfloat16)
    low = (table - high.astype(np.float64)).astype(np.float32).astype(ml_dtypes.bfloat16)
    return high, low


def stacked(table):
    return np.concatenate(halves(table), axis=0)


@functools.cache
def tables():
    sx, ex = sine_basis(BX)
    sy, ey = sine_basis(BY)
    sz, ez = sine_basis(BZ)
    zh, zl = (np.zeros((BZ, CPAD), ml_dtypes.bfloat16) for _ in range(2))
    zh[:, :BZ], zl[:, :BZ] = halves(sz)
    wz1 = np.concatenate([zh[W:-W], zh[W:-W]], axis=0)
    wz2 = np.zeros((2, 2 * CZ, CPAD), ml_dtypes.bfloat16)
    for layer, rows in ((0, slice(BZ - W, BZ)), (1, slice(0, W))):
        wz2[layer, :CZ] = zl[W:-W]
        wz2[layer, CZ : CZ + W] = zh[rows]
        wz2[layer, CZ + W : CZ + 2 * W] = zh[rows]
        wz2[layer, CZ + 2 * W : CZ + 3 * W] = zl[rows]
    eye8, eye4 = np.eye(8), np.eye(4)
    cx = np.stack([stacked(np.kron(sx[parity::2, :HALF], eye8)) for parity in range(2)])
    cxb = np.stack([stacked(np.kron(sx[W:HALF, parity::2], eye8)) for parity in range(2)])
    cy = stacked(np.kron(eye4, sy))
    cyb = stacked(np.kron(eye4, sy[W:-W]))
    wzb = np.zeros((2, CPAD, CZ), ml_dtypes.bfloat16)
    wzb[0, :BZ], wzb[1, :BZ] = halves(sz[:, W:-W])
    inv = np.zeros((2, HALF, BY, CPAD), np.float32)
    for parity in range(2):
        inv[parity, :, :, :BZ] = 1.0 / (
            ex[parity::2][:, None, None] + ey[None, :, None] + ez[None, None, :]
        )
    return wz1, wz2, cx, cy, cyb, cxb, wzb, inv


def split(value):
    high = value.astype(BF16)
    low = (value - high.astype(F32)).astype(BF16)
    return high, low


def mm(left, right):
    return jnp.dot(left, right, preferred_element_type=F32)


def mm_const(const, rows, value):
    high, low = split(value)
    both = mm(const, high)
    return both[:rows] + both[rows:] + mm(const[:rows], low)


def sweep(body, init, count=CX, unroll=2):
    return lax.fori_loop(0, count, body, init, unroll=unroll)


def kernel(sizes, *refs):
    n_gx, n_gy, n_gz = sizes
    (
        pressure, source, saturation, permeability, compress, porosity, rock, well, oil_factor,
        wz1_in, wz2_in, cx_in, cy_in, cyb_in, cxb_in, wzb_in, inv_in,
        pressure_out, residual_out, saturation_out,
        press, src, sat, perm, comp, poro, rocks, wells,
        wz1, wz2, cx, cy, cyb, cxb, wzb, inv,
        mob, frac0, frac1, frac2, oil, direc, sat_b,
        trans_x, trans_y, trans_z, flux_x, flux_y, flux_z, dflux_x, dflux_y, dflux_z,
        outflow, image,
        send1, recv1, send3, recv3, send4, recv4, send5, recv5,
        box, rz_send, rz, rz_all, rxz,
        a_hi, a_lo, a_halo, z1, x1, y1, w1,
        ar_send1, ar_recv1, ar_send2, ar_recv2,
        in_sems, const_sems, out_sems, send_sems, recv_sems,
    ) = refs
    mx, my, layer = lax.axis_index("gx"), lax.axis_index("gy"), lax.axis_index("gz")
    gx_low, gx_high = lax.rem(mx + n_gx - 1, n_gx), lax.rem(mx + 1, n_gx)
    gy_low, gy_high = lax.rem(my + n_gy - 1, n_gy), lax.rem(my + 1, n_gy)
    gz_other = lax.rem(layer + 1, n_gz)
    to_x = ({"gx": gx_low}, {"gx": gx_high})
    to_y = ({"gy": gy_low}, {"gy": gy_high})
    to_z = {"gz": gz_other}

    group1 = [(dx, dz) for dz in range(n_gz) for dx in range(n_gx) if dx or dz]
    peers1 = [
        {"gx": lax.rem(mx + dx, n_gx), "gz": lax.rem(layer + dz, n_gz)} for dx, dz in group1
    ]
    peers2 = [{"gy": lax.rem(my + dy, n_gy)} for dy in range(1, n_gy)]
    barrier = pltpu.get_barrier_semaphore()
    for peer in peers1 + peers2:
        pl.semaphore_signal(barrier, inc=1, device_id=peer, device_id_type=MESH)

    inner = (pl.ds(1, CX), pl.ds(8, CY))
    loads = [
        pltpu.make_async_copy(a, b, in_sems.at[i])
        for i, (a, b) in enumerate(
            (
                (saturation, sat), (permeability, perm), (rock, rocks), (pressure, press.at[inner]),
                (source, src), (compress, comp), (well, wells), (porosity, poro),
            )
        )
    ]
    for copy in loads:
        copy.start()
    const_loads = [
        pltpu.make_async_copy(a, b, const_sems.at[i])
        for i, (a, b) in enumerate(
            (
                (wz1_in, wz1), (wz2_in, wz2), (cx_in, cx), (cy_in, cy), (cyb_in, cyb),
                (cxb_in, cxb), (wzb_in, wzb), (inv_in, inv),
            )
        )
    ]
    for copy in const_loads:
        copy.start()

    used = [0]

    def remote(source_ref, target_ref, device):
        index = used[0]
        used[0] += 1
        return pltpu.make_async_remote_copy(
            src_ref=source_ref,
            dst_ref=target_ref,
            send_sem=send_sems.at[index],
            recv_sem=recv_sems.at[index],
            device_id=device,
            device_id_type=MESH,
        )

    lane = lax.broadcasted_iota(jnp.int32, (CY, CZ), 1)
    cur_lane = jnp.where(layer == 1, CZ - 1, -1)
    nxt_lane = jnp.where(layer == 0, CZ - 1, -1)
    low_lane = jnp.where(layer == 0, 0, -1)

    def upper(value):
        return jnp.where(lane == cur_lane, 0.0, value)

    def lower(value):
        return jnp.where(lane == low_lane, 0.0, pltpu.roll(value, 1, 1))

    def z_pair(value, halo, x):
        halo = pltpu.roll(halo, CZ - 1 - x, 1)
        return (
            jnp.where(lane == cur_lane, halo, value),
            jnp.where(lane == nxt_lane, halo, pltpu.roll(value, CZ - 1, 1)),
        )

    def z_pack(packed, value, x):
        moved = pltpu.roll(value, x + 1 - layer, 1)
        return jnp.where(lane == x, moved, packed)

    def put_rows(buffer, field, value, x):
        buffer[2, pl.ds(field * CX + x, 1), :] = value[0:1]
        buffer[3, pl.ds(field * CX + x, 1), :] = value[CY - 1 : CY]

    def exchange(send, recv, fields, packed):
        for i, field in enumerate(fields):
            span = pl.ds(i * CX, CX)
            send[0, span, :] = field[1, 8 : 8 + CY, :]
            send[1, span, :] = field[CX, 8 : 8 + CY, :]
            send[4, span, :] = packed[i]
        copies = [
            remote(send.at[0], recv.at[1], to_x[0]),
            remote(send.at[1], recv.at[0], to_x[1]),
            remote(send.at[2], recv.at[3], to_y[0]),
            remote(send.at[3], recv.at[2], to_y[1]),
            remote(send.at[4], recv.at[4], to_z),
        ]
        for copy in copies:
            copy.start()
        return copies

    def unpack(recv, fields):
        for i, field in enumerate(fields):
            span = pl.ds(i * CX, CX)
            field[0, 8 : 8 + CY, :] = recv[0, span, :]
            field[CX + 1, 8 : 8 + CY, :] = recv[1, span, :]

    def unpack_rows(recv, i, field, x):
        field[x + 1, 7:8, :] = recv[2, pl.ds(i * CX + x, 1), :]
        field[x + 1, 8 + CY : 9 + CY, :] = recv[3, pl.ds(i * CX + x, 1), :]

    def mid(field, x):
        return field[x, 8 : 8 + CY, :]

    def fraction(sat_vals, oil_vals):
        water = sat_vals * sat_vals
        rest = 1.0 - sat_vals
        inverse = 1.0 / (water + oil_vals * rest * rest)
        return water * inverse, 2.0 * oil_vals * sat_vals * rest * inverse * inverse

    factor = [oil_factor[k] for k in range(8)]
    for copy in loads[:4]:
        copy.wait()
    zero = jnp.zeros((CY, CZ), F32)

    def stage_a(x, carry):
        total, pack_p, pack_m, pack_f = carry
        kind = rocks[x]
        bit0, bit1, bit2 = (kind & 1) == 1, (kind & 2) == 2, (kind & 4) == 4
        pairs = [jnp.where(bit0, factor[2 * k + 1], factor[2 * k]) for k in range(4)]
        oil_vals = jnp.where(
            bit2, jnp.where(bit1, pairs[3], pairs[2]), jnp.where(bit1, pairs[1], pairs[0])
        )
        s = sat[x]
        rest = 1.0 - s
        water = s * s
        total_mob = water + oil_vals * rest * rest
        m = perm[x] * total_mob
        f = water / total_mob
        p = mid(press, x + 1)
        oil[x] = oil_vals
        mob[x + 1, 8 : 8 + CY, :] = m
        frac0[x + 1, 8 : 8 + CY, :] = f
        for i, value in enumerate((p, m, f)):
            put_rows(send1, i, value, x)
        return total + m, z_pack(pack_p, p, x), z_pack(pack_m, m, x), z_pack(pack_f, f, x)

    total, *packed = sweep(stage_a, (zero, zero, zero, zero))
    mean = jnp.sum(jnp.sum(total, axis=0, keepdims=True), axis=1, keepdims=True) * (
        1.0 / (CX * CY * CZ)
    )
    inv_mean = 1.0 / mean

    pl.semaphore_wait(barrier, len(peers1) + len(peers2))
    fields1 = (press, mob, frac0)
    round1 = exchange(send1, recv1, fields1, packed)
    for copy in loads[4:]:
        copy.wait()
    for copy in round1:
        copy.wait()
    unpack(recv1, fields1)
    rz_send[...] = jnp.zeros_like(rz_send)

    def harmonic(a, b):
        return 2.0 * a * b / (a + b)

    def x_face(x):
        tx = harmonic(mid(mob, x), mid(mob, x + 1))
        fx = tx * (mid(press, x) - mid(press, x + 1))
        trans_x[x] = tx
        flux_x[x] = fx
        return fx

    def stage_b(x, before):
        for i, field in enumerate(fields1):
            unpack_rows(recv1, i, field, x)
        fx = x_face(x + 1)
        ty = harmonic(mob[x + 1, 0:40, :], mob[x + 1, 1:41, :])
        fy = ty * (press[x + 1, 0:40, :] - press[x + 1, 1:41, :])
        trans_y[x] = ty
        flux_y[x] = fy
        m = mid(mob, x + 1)
        p = mid(press, x + 1)
        tz = harmonic(*z_pair(m, recv1[4, CX : 2 * CX, :], x))
        p_cur, p_nxt = z_pair(p, recv1[4, 0:CX, :], x)
        fz = tz * (p_cur - p_nxt)
        trans_z[x] = tz
        flux_z[x] = fz
        well_flag = wells[x].astype(F32)
        diag = comp[x] + WELL_INDEX * well_flag * m
        comp[x] = diag
        result = diag * p + (fx - before)
        result = result + (fy[8:40] - flux_y[x, 7:39, :])
        result = result + (upper(fz) - lower(fz))
        r = src[x] - result
        big = x + W
        box[big, W : W + CY, :] = r
        group = big // 16
        place = (big % 16) * 8
        moved = pltpu.roll(r, lax.rem(place + 8 * (1 - layer), CZ), 1)
        kept = rz_send[group, W : W + CY, :]
        rz_send[group, W : W + CY, :] = jnp.where(
            (lane >= place) & (lane < place + 8), moved, kept
        )
        return fx

    sweep(stage_b, x_face(0))

    yspan = pl.ds(W, CY)
    xspan = pl.ds(W, CX)
    low_rows, high_rows = pl.ds(0, W), pl.ds(W + CY, W)
    first_rows, last_rows = pl.ds(W, W), pl.ds(CY, W)
    copy_z = remote(rz_send.at[:, yspan], rz.at[:, yspan], to_z)
    copy_x = [
        remote(box.at[first_rows, yspan], box.at[high_rows, yspan], to_x[0]),
        remote(box.at[last_rows, yspan], box.at[low_rows, yspan], to_x[1]),
    ]
    copy_y = [
        remote(box.at[xspan, first_rows], box.at[xspan, high_rows], to_y[0]),
        remote(box.at[xspan, last_rows], box.at[xspan, low_rows], to_y[1]),
    ]
    copy_xz = [
        remote(rz.at[0, yspan], rxz.at[1], to_x[0]),
        remote(rz.at[2, yspan], rxz.at[0], to_x[1]),
    ]
    copy_xy = [
        remote(box.at[rows, first_rows], box.at[rows, high_rows], to_y[0])
        for rows in (low_rows, high_rows)
    ] + [
        remote(box.at[rows, last_rows], box.at[rows, low_rows], to_y[1])
        for rows in (low_rows, high_rows)
    ]
    copy_yz = [
        remote(rz_all.at[:, first_rows], rz_all.at[:, high_rows], to_y[0]),
        remote(rz_all.at[:, last_rows], rz_all.at[:, low_rows], to_y[1]),
    ]
    for copy in (copy_z, *copy_x, *copy_y):
        copy.start()
    copy_z.wait()
    for copy in copy_xz:
        copy.start()
    for copy in copy_xz:
        copy.wait()
    own_left = lane < CZ // 2
    rz_all[0, W : W + CY, :] = jnp.where(own_left, rxz[0], rz[0, W : W + CY, :])
    rz_all[1, W : W + CY, :] = rz[1, W : W + CY, :]
    rz_all[2, W : W + CY, :] = jnp.where(own_left, rz[2, W : W + CY, :], rxz[1])
    for copy in copy_yz:
        copy.start()
    for copy in copy_x:
        copy.wait()
    for copy in copy_xy:
        copy.start()
    for copy in (*copy_y, *copy_yz, *copy_xy):
        copy.wait()
    for copy in const_loads:
        copy.wait()

    wide_lane = lax.broadcasted_iota(jnp.int32, (BY, CZ), 1)

    def fold(i, carry):
        j = BX - 1 - i
        v, w = box[i], box[j]
        hv = pltpu.roll(rz_all[i // 16], lax.rem(CZ - (i % 16) * 8, CZ), 1)
        hw = pltpu.roll(rz_all[j // 16], lax.rem(CZ - (j % 16) * 8, CZ), 1)
        for parity, (main, halo) in enumerate(((v + w, hv + hw), (v - w, hv - hw))):
            rows = pl.ds(pl.multiple_of((parity * HALF + i) * BY, 16), BY)
            high, low = split(main)
            a_hi[rows, :] = high
            a_lo[rows, :] = low
            halo_high = halo.astype(BF16).astype(F32)
            halo_low = halo - halo_high
            tile = jnp.where(
                wide_lane < 8,
                halo_high,
                jnp.where(
                    wide_lane < 16, pltpu.roll(halo_low, 8, 1), pltpu.roll(halo_high, 16, 1)
                ),
            )
            a_halo[rows, :] = tile.astype(BF16)
        return carry

    sweep(fold, 0, HALF)
    weights2 = wz2[layer]
    for chunk in range(6):
        rows = slice(chunk * 384, (chunk + 1) * 384)
        high = a_hi[rows]
        out = mm(jnp.concatenate([high, a_lo[rows]], axis=1), wz1[...]) + mm(
            jnp.concatenate([high, a_halo[rows]], axis=1), weights2
        )
        z1[chunk // 3, (chunk % 3) * 8 : (chunk % 3) * 8 + 8] = out.reshape(8, BY, CPAD)
    for parity in range(2):
        for block in range(BY // 8):
            rows = slice(block * 8, block * 8 + 8)
            value = z1[parity, :, rows, :].reshape(HALF * 8, CPAD)
            out = mm_const(cx[parity], HALF * 8, value)
            x1[parity, :, rows, :] = out.reshape(HALF, 8, CPAD)
    for parity in range(2):
        for block in range(HALF // 4):
            span = slice(block * 4, block * 4 + 4)
            value = x1[parity, span].reshape(4 * BY, CPAD)
            out = mm_const(cy[...], 4 * BY, value) * inv[parity, span].reshape(4 * BY, CPAD)
            out = mm_const(cyb[...], 4 * CY, out)
            y1[parity, span] = out.reshape(4, CY, CPAD)
    for parity in range(2):
        for block in range(CY // 8):
            rows = slice(block * 8, block * 8 + 8)
            value = y1[parity, :, rows, :].reshape(HALF * 8, CPAD)
            out = mm_const(cxb[parity], KEPT * 8, value)
            w1[parity, :, rows, :] = out.reshape(KEPT, 8, CPAD)
    for block in range(4):
        span = slice(block * 4, block * 4 + 4)
        sides = []
        for parity in range(2):
            high, low = split(w1[parity, span].reshape(4 * CY, CPAD))
            sides.append(mm(high, wzb[0]) + mm(low, wzb[0]) + mm(high, wzb[1]))
        plus = (sides[0] + sides[1]) * inv_mean
        minus = (sides[0] - sides[1]) * inv_mean
        for k in range(4):
            i = block * 4 + k
            direc[1 + i, 8 : 8 + CY, :] = plus[k * CY : (k + 1) * CY]
            direc[CX - i, 8 : 8 + CY, :] = minus[k * CY : (k + 1) * CY]

    def stage_c(x, carry):
        along, pack_d = carry
        d = mid(direc, x + 1)
        put_rows(send3, 0, d, x)
        return along + d * box[x + W, W : W + CY, :], z_pack(pack_d, d, x)

    along, pack_d = sweep(stage_c, (zero, zero))
    round3 = exchange(send3, recv3, (direc,), (pack_d,))
    for copy in round3:
        copy.wait()
    unpack(recv3, (direc,))

    def d_face(x):
        fx = trans_x[x] * (mid(direc, x) - mid(direc, x + 1))
        dflux_x[x] = fx
        return fx

    def stage_d(x, carry):
        before, curve = carry
        unpack_rows(recv3, 0, direc, x)
        fx = d_face(x + 1)
        fy = trans_y[x] * (direc[x + 1, 0:40, :] - direc[x + 1, 1:41, :])
        dflux_y[x] = fy
        d = mid(direc, x + 1)
        d_cur, d_nxt = z_pair(d, recv3[4], x)
        fz = trans_z[x] * (d_cur - d_nxt)
        dflux_z[x] = fz
        result = comp[x] * d + (fx - before)
        result = result + (fy[8:40] - dflux_y[x, 7:39, :])
        result = result + (upper(fz) - lower(fz))
        image[x] = result
        return fx, curve + d * result

    _, curve = sweep(stage_d, (d_face(0), zero))

    ar_send1[...] = jnp.concatenate(
        [
            jnp.broadcast_to(jnp.sum(value, axis=0, keepdims=True), (4, CZ))
            for value in (along, curve)
        ],
        axis=0,
    )
    for send, recv, peers in ((ar_send1, ar_recv1, peers1), (ar_send2, ar_recv2, peers2)):
        copies = [remote(send, recv.at[i], peer) for i, peer in enumerate(peers)]
        for copy in copies:
            copy.start()
        for copy in copies:
            copy.wait()
        result = send[...]
        for i in range(len(peers)):
            result = result + recv[i]
        if send is ar_send1:
            ar_send2[...] = result
    sums = jnp.sum(result, axis=1, keepdims=True)
    step = sums[0:1] / sums[4:5]

    def total_x(x):
        fx = flux_x[x] + step * dflux_x[x]
        flux_x[x] = fx
        return fx, upwind_x(frac0, fx, x)

    def upwind_x(frac, fx, x):
        return fx * jnp.where(fx > 0.0, mid(frac, x), mid(frac, x + 1))

    def balance_of(frac, recv, field, fx_flow, flow_before, x, sat_vals):
        fy_low, fy_high = flux_y[x, 7:39, :], flux_y[x, 8:40, :]
        f = mid(frac, x + 1)
        flow_low = fy_low * jnp.where(fy_low > 0.0, frac[x + 1, 7:39, :], f)
        flow_high = fy_high * jnp.where(fy_high > 0.0, f, frac[x + 1, 9:41, :])
        f_cur, f_nxt = z_pair(f, recv[4, field * CX : (field + 1) * CX, :], x)
        fz = flux_z[x]
        flow_z = fz * jnp.where(fz > 0.0, f_cur, f_nxt)
        balance = (fx_flow - flow_before) + (flow_high - flow_low)
        balance = balance + (upper(flow_z) - lower(flow_z))
        return balance - INJECT_RATE * wells[x].astype(F32)

    def update(balance, storage, out_vals, sat_vals, oil_vals):
        _, slope = fraction(sat_vals, oil_vals)
        return sat_vals - balance / (storage + out_vals * jnp.abs(slope))

    def stage_e(x, carry):
        fx_before, flow_before, pack_f = carry
        d = mid(direc, x + 1)
        press[x + 1, 8 : 8 + CY, :] = mid(press, x + 1) + step * d
        src[x] = box[x + W, W : W + CY, :] - step * image[x]
        fx, flow = total_x(x + 1)
        flux_y[x] = flux_y[x] + step * dflux_y[x]
        fz = flux_z[x] + step * dflux_z[x]
        flux_z[x] = fz
        out_vals = jnp.maximum(fx, 0.0) + jnp.maximum(-fx_before, 0.0)
        out_vals = out_vals + jnp.maximum(flux_y[x, 8:40, :], 0.0)
        out_vals = out_vals + jnp.maximum(-flux_y[x, 7:39, :], 0.0)
        out_vals = out_vals + jnp.maximum(upper(fz), 0.0) + jnp.maximum(-lower(fz), 0.0)
        outflow[x] = out_vals
        storage = poro[x] / TIME_STEP
        s = sat[x]
        balance = balance_of(frac0, recv1, 2, flow, flow_before, x, s)
        s_new = update(balance, storage, out_vals, s, oil[x])
        sat_b[x] = s_new
        f_new, _ = fraction(s_new, oil[x])
        frac1[x + 1, 8 : 8 + CY, :] = f_new
        put_rows(send4, 0, f_new, x)
        return fx, flow, z_pack(pack_f, f_new, x)

    fx, flow = total_x(0)
    _, _, pack_f = sweep(stage_e, (fx, flow, zero))
    round4 = exchange(send4, recv4, (frac1,), (pack_f,))
    stores = [
        pltpu.make_async_copy(press.at[inner], pressure_out, out_sems.at[0]),
        pltpu.make_async_copy(src, residual_out, out_sems.at[1]),
    ]
    for copy in stores:
        copy.start()
    for copy in round4:
        copy.wait()
    unpack(recv4, (frac1,))

    def later(frac, recv, last, x, carry):
        flow_before, pack_f = carry
        unpack_rows(recv, 0, frac, x)
        flow = upwind_x(frac, flux_x[x + 1], x + 1)
        storage = poro[x] / TIME_STEP
        s = sat_b[x]
        balance = balance_of(frac, recv, 0, flow, flow_before, x, s)
        balance = balance + storage * (s - sat[x])
        s_new = update(balance, storage, outflow[x], s, oil[x])
        sat_b[x] = s_new
        if not last:
            f_new, _ = fraction(s_new, oil[x])
            frac2[x + 1, 8 : 8 + CY, :] = f_new
            put_rows(send5, 0, f_new, x)
            pack_f = z_pack(pack_f, f_new, x)
        return flow, pack_f

    flow = upwind_x(frac1, flux_x[0], 0)
    _, pack_f = sweep(functools.partial(later, frac1, recv4, False), (flow, zero))
    round5 = exchange(send5, recv5, (frac2,), (pack_f,))
    for copy in round5:
        copy.wait()
    unpack(recv5, (frac2,))
    flow = upwind_x(frac2, flux_x[0], 0)
    sweep(functools.partial(later, frac2, recv5, True), (flow, zero))
    last_store = pltpu.make_async_copy(sat_b, saturation_out, out_sems.at[2])
    last_store.start()
    for copy in (*stores, last_store):
        copy.wait()


def per_device(sizes, *args):
    consts = tables()
    brick = pltpu.VMEM((CX, CY, CZ), F32)
    bricki = pltpu.VMEM((CX, CY, CZ), jnp.int32)
    padded = pltpu.VMEM((CX + 2, BY, CZ), F32)
    faces_x = pltpu.VMEM((CX + 1, CY, CZ), F32)
    faces_y = pltpu.VMEM((CX, 40, CZ), F32)

    def buffers(fields):
        return [pltpu.VMEM((5, fields * CX, CZ), F32)] * 2

    rows = 2 * HALF * BY
    n1 = sizes[0] * sizes[2] - 1
    n2 = sizes[1] - 1
    tile = pltpu.VMEM((8, CZ), F32)
    n_remote = 5 * 4 + 13 + n1 + n2
    scratch = (
        [padded, brick, brick, brick, brick, brick, bricki, bricki]
        + [pltpu.VMEM(c.shape, c.dtype) for c in consts]
        + [padded] * 4
        + [brick, padded, brick]
        + [faces_x, faces_y, brick] * 3
        + [brick] * 2
        + buffers(3)
        + buffers(1) * 3
        + [pltpu.VMEM((BX, BY, CZ), F32)]
        + [pltpu.VMEM((3, BY, CZ), F32)] * 3
        + [pltpu.VMEM((2, CY, CZ), F32)]
        + [pltpu.VMEM((rows, CZ), BF16)] * 3
        + [pltpu.VMEM((2, HALF, BY, CPAD), F32)] * 2
        + [pltpu.VMEM((2, HALF, CY, CPAD), F32), pltpu.VMEM((2, KEPT, CY, CPAD), F32)]
        + [tile, pltpu.VMEM((n1, 8, CZ), F32), tile, pltpu.VMEM((n2, 8, CZ), F32)]
        + [pltpu.SemaphoreType.DMA((8,)), pltpu.SemaphoreType.DMA((8,))]
        + [pltpu.SemaphoreType.DMA((3,))]
        + [pltpu.SemaphoreType.DMA((n_remote,))] * 2
    )
    anywhere = pl.BlockSpec(memory_space=pl.ANY)
    in_specs = [anywhere] * 8 + [pl.BlockSpec(memory_space=pltpu.SMEM)] + [anywhere] * len(consts)
    return pl.pallas_call(
        functools.partial(kernel, sizes),
        out_shape=[jax.ShapeDtypeStruct((CX, CY, CZ), F32)] * 3,
        in_specs=in_specs,
        out_specs=[anywhere] * 3,
        scratch_shapes=scratch,
        compiler_params=pltpu.CompilerParams(
            collective_id=0, has_side_effects=True, vmem_limit_bytes=60 * 1024 * 1024
        ),
    )(*args, *(jnp.asarray(c) for c in consts))


def solution(mesh):
    sizes = tuple(mesh.shape[axis] for axis in ("gx", "gy", "gz"))
    spec = P("gx", "gy", "gz")
    return jax.shard_map(
        functools.partial(per_device, sizes),
        mesh=mesh,
        in_specs=(spec,) * 8 + (P(),),
        out_specs=(spec,) * 3,
        check_vma=False,
    )
```

profile of v0, /device:TPU:0, one launch (start us, length us, event | category | flops | bytes accessed | tf_op | source)
XLA Modules:
  0.0 80.1 jit_solution(6022761821096327821)
XLA Ops:
  0.6 74.9 %shard_map.184 = (f32[32,32,128]{2,1,0:T(8,128)}, f32[32,32,128]{2,1,0:T(8,128)}, f32[32,32,128]{2,1,0:T(8,128)}) custom-call(f32[32,32,128]{2,1,0:T(8,128)} %refs_0_.1, f32[32,32,128]{2,1,0:T(8,128)} %refs_1_.1, f32[32,32,128]{2,1,0:T(8,128)} %refs_2_.1, f32[32,32,128]{2,1,0:T(8,128)} %refs_3_.1, f32[32,32,128]{2,1,0:T(8,128)} %refs_4_.1, ...), custom_call_target="tpu_custom_call" | custom-call | tf_op jit(solution)/shard_map/pallas_call | solution.py:619
  75.5 0.0 copy-start
  75.5 1.9 %copy.23 = f32[32,32,128]{2,1,0:T(8,128)} copy(f32[32,32,128]{2,1,0:T(8,128)} %get-tuple-element.6) | data formatting | bytes 1048576
  77.4 1.9 %copy.24 = f32[32,32,128]{2,1,0:T(8,128)} copy(f32[32,32,128]{2,1,0:T(8,128)} %get-tuple-element.7) | data formatting | bytes 1048576
  79.3 0.0 copy-done
  79.3 0.8 copy.25
Async XLA Ops:
  75.5 3.8 %copy-start = (f32[32,32,128]{2,1,0:T(8,128)S(1)}, f32[32,32,128]{2,1,0:T(8,128)}, u32[]{:S(2)}) copy-start(f32[32,32,128]{2,1,0:T(8,128)} %get-tuple-element.8) | copy-start | bytes 1572868
where the time goes:
time: 80.3 us; the launch traced here: 80.1 us
  Pallas kernels  74.9 us (93%)
  local copies, waits for them, and re-layouts  4.59 us (6%)
    pallas_call x1, Pallas kernels, per_device(): pl.pallas_call(functools.partial(kernel, sizes), out_shape=[jax.ShapeDtyp...  74.9 us
    unnamed x5, local copies, waits for them, and re-layouts  4.59 us

commit v1 on v0

--- a/solution.py
+++ b/solution.py
@@ -107,24 +107,26 @@
         send1, recv1, send3, recv3, send4, recv4, send5, recv5,
         box, rz_send, rz, rz_all, rxz,
         a_hi, a_lo, a_halo, z1, x1, y1, w1,
+        face_t, face_p, face_d, face_o, face_f,
         ar_send1, ar_recv1, ar_send2, ar_recv2,
         in_sems, const_sems, out_sems, send_sems, recv_sems,
     ) = refs
     mx, my, layer = lax.axis_index("gx"), lax.axis_index("gy"), lax.axis_index("gz")
-    gx_low, gx_high = lax.rem(mx + n_gx - 1, n_gx), lax.rem(mx + 1, n_gx)
-    gy_low, gy_high = lax.rem(my + n_gy - 1, n_gy), lax.rem(my + 1, n_gy)
-    gz_other = lax.rem(layer + 1, n_gz)
-    to_x = ({"gx": gx_low}, {"gx": gx_high})
-    to_y = ({"gy": gy_low}, {"gy": gy_high})
-    to_z = {"gz": gz_other}
-
-    group1 = [(dx, dz) for dz in range(n_gz) for dx in range(n_gx) if dx or dz]
-    peers1 = [
-        {"gx": lax.rem(mx + dx, n_gx), "gz": lax.rem(layer + dz, n_gz)} for dx, dz in group1
-    ]
-    peers2 = [{"gy": lax.rem(my + dy, n_gy)} for dy in range(1, n_gy)]
+
+    def device(dx, dy, dz):
+        return {
+            "gx": lax.rem(mx + n_gx + dx, n_gx),
+            "gy": lax.rem(my + n_gy + dy, n_gy),
+            "gz": lax.rem(layer + n_gz + dz, n_gz),
+        }
+
+    peers1 = [device(dx, 0, dz) for dz in range(n_gz) for dx in range(n_gx) if dx or dz]
+    peers2 = [device(0, dy, 0) for dy in range(1, n_gy)]
+    steps = (-1, 0, 1)
+    diagonal = [device(dx, dy, dz) for dz in (0, 1) for dx in steps for dy in steps if dy and (dx or dz)]
+    everyone = peers1 + peers2 + diagonal
     barrier = pltpu.get_barrier_semaphore()
-    for peer in peers1 + peers2:
+    for peer in everyone:
         pl.semaphore_signal(barrier, inc=1, device_id=peer, device_id_type=MESH)
 
     inner = (pl.ds(1, CX), pl.ds(8, CY))
@@ -153,7 +155,7 @@
 
     used = [0]
 
-    def remote(source_ref, target_ref, device):
+    def remote(source_ref, target_ref, target):
         index = used[0]
         used[0] += 1
         return pltpu.make_async_remote_copy(
@@ -161,31 +163,17 @@
             dst_ref=target_ref,
             send_sem=send_sems.at[index],
             recv_sem=recv_sems.at[index],
-            device_id=device,
+            device_id=target,
             device_id_type=MESH,
         )
 
     lane = lax.broadcasted_iota(jnp.int32, (CY, CZ), 1)
-    cur_lane = jnp.where(layer == 1, CZ - 1, -1)
-    nxt_lane = jnp.where(layer == 0, CZ - 1, -1)
-    low_lane = jnp.where(layer == 0, 0, -1)
-
-    def upper(value):
-        return jnp.where(lane == cur_lane, 0.0, value)
-
-    def lower(value):
-        return jnp.where(lane == low_lane, 0.0, pltpu.roll(value, 1, 1))
-
-    def z_pair(value, halo, x):
-        halo = pltpu.roll(halo, CZ - 1 - x, 1)
-        return (
-            jnp.where(lane == cur_lane, halo, value),
-            jnp.where(lane == nxt_lane, halo, pltpu.roll(value, CZ - 1, 1)),
-        )
+    row8 = lax.broadcasted_iota(jnp.int32, (8, CZ), 0)
+    face_lane = jnp.where(layer == 0, CZ - 1, 0)
+    zero = jnp.zeros((CY, CZ), F32)
 
     def z_pack(packed, value, x):
-        moved = pltpu.roll(value, x + 1 - layer, 1)
-        return jnp.where(lane == x, moved, packed)
+        return jnp.where(lane == x, pltpu.roll(value, x + 1 - layer, 1), packed)
 
     def put_rows(buffer, field, value, x):
         buffer[2, pl.ds(field * CX + x, 1), :] = value[0:1]
@@ -198,25 +186,26 @@
             send[1, span, :] = field[CX, 8 : 8 + CY, :]
             send[4, span, :] = packed[i]
         copies = [
-            remote(send.at[0], recv.at[1], to_x[0]),
-            remote(send.at[1], recv.at[0], to_x[1]),
-            remote(send.at[2], recv.at[3], to_y[0]),
-            remote(send.at[3], recv.at[2], to_y[1]),
-            remote(send.at[4], recv.at[4], to_z),
+            remote(send.at[2], recv.at[3], device(0, -1, 0)),
+            remote(send.at[3], recv.at[2], device(0, 1, 0)),
+            remote(send.at[0], recv.at[1], device(-1, 0, 0)),
+            remote(send.at[1], recv.at[0], device(1, 0, 0)),
+            remote(send.at[4], recv.at[4], device(0, 0, 1)),
         ]
         for copy in copies:
             copy.start()
         return copies
 
-    def unpack(recv, fields):
-        for i, field in enumerate(fields):
-            span = pl.ds(i * CX, CX)
-            field[0, 8 : 8 + CY, :] = recv[0, span, :]
-            field[CX + 1, 8 : 8 + CY, :] = recv[1, span, :]
-
-    def unpack_rows(recv, i, field, x):
-        field[x + 1, 7:8, :] = recv[2, pl.ds(i * CX + x, 1), :]
-        field[x + 1, 8 + CY : 9 + CY, :] = recv[3, pl.ds(i * CX + x, 1), :]
+    def part(buffer, field):
+        return [buffer[k, field * CX : (field + 1) * CX, :] for k in range(5)]
+
+    def at_faces(faces, x):
+        value = jnp.where(x == 0, faces[0], 0.0) + jnp.where(x == CX - 1, faces[1], 0.0)
+        moved = pltpu.roll(faces[4], lax.rem(CZ - 1 - x + layer, CZ), 1)
+        value = value + jnp.where(lane == face_lane, moved, 0.0)
+        first = value[0:8] + jnp.where(row8 == 0, faces[2, pl.ds(x, 1), :], 0.0)
+        last = value[CY - 8 : CY] + jnp.where(row8 == 7, faces[3, pl.ds(x, 1), :], 0.0)
+        return jnp.concatenate([first, value[8 : CY - 8], last], axis=0)
 
     def mid(field, x):
         return field[x, 8 : 8 + CY, :]
@@ -227,10 +216,25 @@
         inverse = 1.0 / (water + oil_vals * rest * rest)
         return water * inverse, 2.0 * oil_vals * sat_vals * rest * inverse * inverse
 
+    def upwind(flux, here, there):
+        return flux * jnp.where(flux > 0.0, here, there)
+
+    for field in (mob, press, direc, frac0, frac1, frac2):
+        field[0] = jnp.zeros((BY, CZ), F32)
+        field[CX + 1] = jnp.zeros((BY, CZ), F32)
+
+    def clear(x, carry):
+        for field in (mob, press, direc, frac0, frac1, frac2):
+            field[x + 1, 0:8, :] = zero[0:8]
+            field[x + 1, 8 + CY : BY, :] = zero[0:8]
+        return carry
+
+    sweep(clear, 0)
+    rz_send[...] = jnp.zeros_like(rz_send)
+
     factor = [oil_factor[k] for k in range(8)]
     for copy in loads[:4]:
         copy.wait()
-    zero = jnp.zeros((CY, CZ), F32)
 
     def stage_a(x, carry):
         total, pack_p, pack_m, pack_f = carry
@@ -260,15 +264,10 @@
     )
     inv_mean = 1.0 / mean
 
-    pl.semaphore_wait(barrier, len(peers1) + len(peers2))
-    fields1 = (press, mob, frac0)
-    round1 = exchange(send1, recv1, fields1, packed)
+    pl.semaphore_wait(barrier, len(everyone))
+    round1 = exchange(send1, recv1, (press, mob, frac0), packed)
     for copy in loads[4:]:
         copy.wait()
-    for copy in round1:
-        copy.wait()
-    unpack(recv1, fields1)
-    rz_send[...] = jnp.zeros_like(rz_send)
 
     def harmonic(a, b):
         return 2.0 * a * b / (a + b)
@@ -281,8 +280,6 @@
         return fx
 
     def stage_b(x, before):
-        for i, field in enumerate(fields1):
-            unpack_rows(recv1, i, field, x)
         fx = x_face(x + 1)
         ty = harmonic(mob[x + 1, 0:40, :], mob[x + 1, 1:41, :])
         fy = ty * (press[x + 1, 0:40, :] - press[x + 1, 1:41, :])
@@ -290,19 +287,33 @@
         flux_y[x] = fy
         m = mid(mob, x + 1)
         p = mid(press, x + 1)
-        tz = harmonic(*z_pair(m, recv1[4, CX : 2 * CX, :], x))
-        p_cur, p_nxt = z_pair(p, recv1[4, 0:CX, :], x)
-        fz = tz * (p_cur - p_nxt)
+        tz = jnp.where(lane == CZ - 1, 0.0, harmonic(m, pltpu.roll(m, CZ - 1, 1)))
+        fz = tz * (p - pltpu.roll(p, CZ - 1, 1))
         trans_z[x] = tz
         flux_z[x] = fz
-        well_flag = wells[x].astype(F32)
-        diag = comp[x] + WELL_INDEX * well_flag * m
+        diag = comp[x] + WELL_INDEX * wells[x].astype(F32) * m
         comp[x] = diag
         result = diag * p + (fx - before)
         result = result + (fy[8:40] - flux_y[x, 7:39, :])
-        result = result + (upper(fz) - lower(fz))
-        r = src[x] - result
+        result = result + (fz - pltpu.roll(fz, 1, 1))
+        box[x + W, W : W + CY, :] = src[x] - result
+        return fx
+
+    sweep(stage_b, x_face(0))
+    for copy in round1:
+        copy.wait()
+    for k in range(5):
+        own_p, own_m = (send1[k, i * CX : (i + 1) * CX, :] for i in range(2))
+        far_p, far_m = (recv1[k, i * CX : (i + 1) * CX, :] for i in range(2))
+        tk = harmonic(own_m, far_m)
+        if k == 4:
+            tk = jnp.where(lane < CX, tk, 0.0)
+        face_t[k] = tk
+        face_p[k] = tk * (own_p - far_p)
+
+    def stage_r(x, carry):
         big = x + W
+        r = box[big, W : W + CY, :] - at_faces(face_p, x)
         box[big, W : W + CY, :] = r
         group = big // 16
         place = (big % 16) * 8
@@ -311,60 +322,38 @@
         rz_send[group, W : W + CY, :] = jnp.where(
             (lane >= place) & (lane < place + 8), moved, kept
         )
-        return fx
-
-    sweep(stage_b, x_face(0))
-
-    yspan = pl.ds(W, CY)
-    xspan = pl.ds(W, CX)
-    low_rows, high_rows = pl.ds(0, W), pl.ds(W + CY, W)
-    first_rows, last_rows = pl.ds(W, W), pl.ds(CY, W)
-    copy_z = remote(rz_send.at[:, yspan], rz.at[:, yspan], to_z)
-    copy_x = [
-        remote(box.at[first_rows, yspan], box.at[high_rows, yspan], to_x[0]),
-        remote(box.at[last_rows, yspan], box.at[low_rows, yspan], to_x[1]),
-    ]
-    copy_y = [
-        remote(box.at[xspan, first_rows], box.at[xspan, high_rows], to_y[0]),
-        remote(box.at[xspan, last_rows], box.at[xspan, low_rows], to_y[1]),
-    ]
-    copy_xz = [
-        remote(rz.at[0, yspan], rxz.at[1], to_x[0]),
-        remote(rz.at[2, yspan], rxz.at[0], to_x[1]),
-    ]
-    copy_xy = [
-        remote(box.at[rows, first_rows], box.at[rows, high_rows], to_y[0])
-        for rows in (low_rows, high_rows)
-    ] + [
-        remote(box.at[rows, last_rows], box.at[rows, low_rows], to_y[1])
-        for rows in (low_rows, high_rows)
-    ]
-    copy_yz = [
-        remote(rz_all.at[:, first_rows], rz_all.at[:, high_rows], to_y[0]),
-        remote(rz_all.at[:, last_rows], rz_all.at[:, low_rows], to_y[1]),
-    ]
-    for copy in (copy_z, *copy_x, *copy_y):
+        return carry
+
+    inside = pl.ds(W, CX)
+    cut = {-1: (pl.ds(W, W), pl.ds(W + CX, W)), 0: (inside, inside), 1: (pl.ds(CX, W), pl.ds(0, W))}
+    wide_copies, far_copies = [], []
+    for dx in (-1, 1, 0):
+        for dy in (0, -1, 1):
+            (sx, tx), (sy, ty) = cut[dx], cut[dy]
+            if dx or dy:
+                wide_copies.append(remote(box.at[sx, sy], box.at[tx, ty], device(dx, dy, 0)))
+            if dx:
+                mine, theirs = (0, 1) if dx < 0 else (2, 0)
+                source_ref, target_ref = rz_send.at[mine, sy], rxz.at[theirs, ty]
+            else:
+                source_ref, target_ref = rz_send.at[:, sy], rz.at[:, ty]
+            far_copies.append(remote(source_ref, target_ref, device(dx, dy, 1)))
+    for k in range(2):
+        lax.fori_loop(24 * k, 24 * k + 8, stage_r, 0, unroll=2)
+        for copy in wide_copies[3 * k : 3 * k + 3]:
+            copy.start()
+    lax.fori_loop(8, 24, stage_r, 0, unroll=2)
+    for copy in wide_copies[6:] + far_copies:
         copy.start()
-    copy_z.wait()
-    for copy in copy_xz:
-        copy.start()
-    for copy in copy_xz:
-        copy.wait()
-    own_left = lane < CZ // 2
-    rz_all[0, W : W + CY, :] = jnp.where(own_left, rxz[0], rz[0, W : W + CY, :])
-    rz_all[1, W : W + CY, :] = rz[1, W : W + CY, :]
-    rz_all[2, W : W + CY, :] = jnp.where(own_left, rz[2, W : W + CY, :], rxz[1])
-    for copy in copy_yz:
-        copy.start()
-    for copy in copy_x:
-        copy.wait()
-    for copy in copy_xy:
-        copy.start()
-    for copy in (*copy_y, *copy_yz, *copy_xy):
+    for copy in wide_copies + far_copies:
         copy.wait()
     for copy in const_loads:
         copy.wait()
 
+    own_left = lax.broadcasted_iota(jnp.int32, (BY, CZ), 1) < CZ // 2
+    rz_all[0] = jnp.where(own_left, rxz[0], rz[0])
+    rz_all[1] = rz[1]
+    rz_all[2] = jnp.where(own_left, rz[2], rxz[1])
     wide_lane = lax.broadcasted_iota(jnp.int32, (BY, CZ), 1)
 
     def fold(i, carry):
@@ -389,7 +378,7 @@
             a_halo[rows, :] = tile.astype(BF16)
         return carry
 
-    sweep(fold, 0, HALF)
+    sweep(fold, 0, HALF, 4)
     weights2 = wz2[layer]
     for chunk in range(6):
         rows = slice(chunk * 384, (chunk + 1) * 384)
@@ -409,7 +398,11 @@
             span = slice(block * 4, block * 4 + 4)
             value = x1[parity, span].reshape(4 * BY, CPAD)
             out = mm_const(cy[...], 4 * BY, value) * inv[parity, span].reshape(4 * BY, CPAD)
-            out = mm_const(cyb[...], 4 * CY, out)
+            z1[parity, span] = out.reshape(4, BY, CPAD)
+    for parity in range(2):
+        for block in range(HALF // 4):
+            span = slice(block * 4, block * 4 + 4)
+            out = mm_const(cyb[...], 4 * CY, z1[parity, span].reshape(4 * BY, CPAD))
             y1[parity, span] = out.reshape(4, CY, CPAD)
     for parity in range(2):
         for block in range(CY // 8):
@@ -438,9 +431,6 @@
 
     along, pack_d = sweep(stage_c, (zero, zero))
     round3 = exchange(send3, recv3, (direc,), (pack_d,))
-    for copy in round3:
-        copy.wait()
-    unpack(recv3, (direc,))
 
     def d_face(x):
         fx = trans_x[x] * (mid(direc, x) - mid(direc, x + 1))
@@ -449,21 +439,25 @@
 
     def stage_d(x, carry):
         before, curve = carry
-        unpack_rows(recv3, 0, direc, x)
         fx = d_face(x + 1)
         fy = trans_y[x] * (direc[x + 1, 0:40, :] - direc[x + 1, 1:41, :])
         dflux_y[x] = fy
         d = mid(direc, x + 1)
-        d_cur, d_nxt = z_pair(d, recv3[4], x)
-        fz = trans_z[x] * (d_cur - d_nxt)
+        fz = trans_z[x] * (d - pltpu.roll(d, CZ - 1, 1))
         dflux_z[x] = fz
         result = comp[x] * d + (fx - before)
         result = result + (fy[8:40] - dflux_y[x, 7:39, :])
-        result = result + (upper(fz) - lower(fz))
+        result = result + (fz - pltpu.roll(fz, 1, 1))
         image[x] = result
         return fx, curve + d * result
 
     _, curve = sweep(stage_d, (d_face(0), zero))
+    for copy in round3:
+        copy.wait()
+    for k in range(5):
+        fd = face_t[k] * (send3[k] - recv3[k])
+        face_d[k] = fd
+        curve = curve + send3[k] * fd
 
     ar_send1[...] = jnp.concatenate(
         [
@@ -472,10 +466,17 @@
         ],
         axis=0,
     )
+
+    def finish_image(x, carry):
+        image[x] = image[x] + at_faces(face_d, x)
+        return carry
+
     for send, recv, peers in ((ar_send1, ar_recv1, peers1), (ar_send2, ar_recv2, peers2)):
         copies = [remote(send, recv.at[i], peer) for i, peer in enumerate(peers)]
         for copy in copies:
             copy.start()
+        if send is ar_send1:
+            sweep(finish_image, 0)
         for copy in copies:
             copy.wait()
         result = send[...]
@@ -486,29 +487,30 @@
     sums = jnp.sum(result, axis=1, keepdims=True)
     step = sums[0:1] / sums[4:5]
 
+    own_f, far_f = part(send1, 2), part(recv1, 2)
+    for k in range(5):
+        flux = face_p[k] + step * face_d[k]
+        face_p[k] = flux
+        face_o[k] = jnp.maximum(flux, 0.0)
+        face_f[k] = upwind(flux, own_f[k], far_f[k])
+
     def total_x(x):
         fx = flux_x[x] + step * dflux_x[x]
         flux_x[x] = fx
-        return fx, upwind_x(frac0, fx, x)
-
-    def upwind_x(frac, fx, x):
-        return fx * jnp.where(fx > 0.0, mid(frac, x), mid(frac, x + 1))
-
-    def balance_of(frac, recv, field, fx_flow, flow_before, x, sat_vals):
-        fy_low, fy_high = flux_y[x, 7:39, :], flux_y[x, 8:40, :]
+        return fx, upwind(fx, mid(frac0, x), mid(frac0, x + 1))
+
+    def balance_of(frac, fx_flow, flow_before, x):
         f = mid(frac, x + 1)
-        flow_low = fy_low * jnp.where(fy_low > 0.0, frac[x + 1, 7:39, :], f)
-        flow_high = fy_high * jnp.where(fy_high > 0.0, f, frac[x + 1, 9:41, :])
-        f_cur, f_nxt = z_pair(f, recv[4, field * CX : (field + 1) * CX, :], x)
-        fz = flux_z[x]
-        flow_z = fz * jnp.where(fz > 0.0, f_cur, f_nxt)
+        flow_low = upwind(flux_y[x, 7:39, :], frac[x + 1, 7:39, :], f)
+        flow_high = upwind(flux_y[x, 8:40, :], f, frac[x + 1, 9:41, :])
+        flow_z = upwind(flux_z[x], f, pltpu.roll(f, CZ - 1, 1))
         balance = (fx_flow - flow_before) + (flow_high - flow_low)
-        balance = balance + (upper(flow_z) - lower(flow_z))
+        balance = balance + (flow_z - pltpu.roll(flow_z, 1, 1))
         return balance - INJECT_RATE * wells[x].astype(F32)
 
-    def update(balance, storage, out_vals, sat_vals, oil_vals):
+    def inverse_of(storage, out_vals, sat_vals, oil_vals):
         _, slope = fraction(sat_vals, oil_vals)
-        return sat_vals - balance / (storage + out_vals * jnp.abs(slope))
+        return 1.0 / (storage + out_vals * jnp.abs(slope))
 
     def stage_e(x, carry):
         fx_before, flow_before, pack_f = carry
@@ -522,12 +524,12 @@
         out_vals = jnp.maximum(fx, 0.0) + jnp.maximum(-fx_before, 0.0)
         out_vals = out_vals + jnp.maximum(flux_y[x, 8:40, :], 0.0)
         out_vals = out_vals + jnp.maximum(-flux_y[x, 7:39, :], 0.0)
-        out_vals = out_vals + jnp.maximum(upper(fz), 0.0) + jnp.maximum(-lower(fz), 0.0)
+        out_vals = out_vals + jnp.maximum(fz, 0.0) + jnp.maximum(-pltpu.roll(fz, 1, 1), 0.0)
+        out_vals = out_vals + at_faces(face_o, x)
         outflow[x] = out_vals
-        storage = poro[x] / TIME_STEP
         s = sat[x]
-        balance = balance_of(frac0, recv1, 2, flow, flow_before, x, s)
-        s_new = update(balance, storage, out_vals, s, oil[x])
+        balance = balance_of(frac0, flow, flow_before, x) + at_faces(face_f, x)
+        s_new = s - balance * inverse_of(poro[x] / TIME_STEP, out_vals, s, oil[x])
         sat_b[x] = s_new
         f_new, _ = fraction(s_new, oil[x])
         frac1[x + 1, 8 : 8 + CY, :] = f_new
@@ -543,35 +545,38 @@
     ]
     for copy in stores:
         copy.start()
-    for copy in round4:
-        copy.wait()
-    unpack(recv4, (frac1,))
-
-    def later(frac, recv, last, x, carry):
-        flow_before, pack_f = carry
-        unpack_rows(recv, 0, frac, x)
-        flow = upwind_x(frac, flux_x[x + 1], x + 1)
+
+    def within(frac, x, flow_before):
+        flow = upwind(flux_x[x + 1], mid(frac, x + 1), mid(frac, x + 2))
         storage = poro[x] / TIME_STEP
         s = sat_b[x]
-        balance = balance_of(frac, recv, 0, flow, flow_before, x, s)
-        balance = balance + storage * (s - sat[x])
-        s_new = update(balance, storage, outflow[x], s, oil[x])
+        balance = balance_of(frac, flow, flow_before, x) + storage * (s - sat[x])
+        inverse = inverse_of(storage, outflow[x], s, oil[x])
+        image[x] = inverse
+        sat_b[x] = s - balance * inverse
+        return flow
+
+    def across(last, x, pack_f):
+        s_new = sat_b[x] - at_faces(face_f, x) * image[x]
         sat_b[x] = s_new
-        if not last:
-            f_new, _ = fraction(s_new, oil[x])
-            frac2[x + 1, 8 : 8 + CY, :] = f_new
-            put_rows(send5, 0, f_new, x)
-            pack_f = z_pack(pack_f, f_new, x)
-        return flow, pack_f
-
-    flow = upwind_x(frac1, flux_x[0], 0)
-    _, pack_f = sweep(functools.partial(later, frac1, recv4, False), (flow, zero))
+        if last:
+            return pack_f
+        f_new, _ = fraction(s_new, oil[x])
+        frac2[x + 1, 8 : 8 + CY, :] = f_new
+        put_rows(send5, 0, f_new, x)
+        return z_pack(pack_f, f_new, x)
+
+    def later(frac, send, recv, copies, last):
+        sweep(functools.partial(within, frac), zero)
+        for copy in copies:
+            copy.wait()
+        for k in range(5):
+            face_f[k] = upwind(face_p[k], send[k], recv[k])
+        return sweep(functools.partial(across, last), zero)
+
+    pack_f = later(frac1, send4, recv4, round4, False)
     round5 = exchange(send5, recv5, (frac2,), (pack_f,))
-    for copy in round5:
-        copy.wait()
-    unpack(recv5, (frac2,))
-    flow = upwind_x(frac2, flux_x[0], 0)
-    sweep(functools.partial(later, frac2, recv5, True), (flow, zero))
+    later(frac2, send5, recv5, round5, True)
     last_store = pltpu.make_async_copy(sat_b, saturation_out, out_sems.at[2])
     last_store.start()
     for copy in (*stores, last_store):
@@ -593,7 +598,7 @@
     n1 = sizes[0] * sizes[2] - 1
     n2 = sizes[1] - 1
     tile = pltpu.VMEM((8, CZ), F32)
-    n_remote = 5 * 4 + 13 + n1 + n2
+    n_remote = 5 * 4 + 17 + n1 + n2
     scratch = (
         [padded, brick, brick, brick, brick, brick, bricki, bricki]
         + [pltpu.VMEM(c.shape, c.dtype) for c in consts]
@@ -605,10 +610,11 @@
         + buffers(1) * 3
         + [pltpu.VMEM((BX, BY, CZ), F32)]
         + [pltpu.VMEM((3, BY, CZ), F32)] * 3
-        + [pltpu.VMEM((2, CY, CZ), F32)]
+        + [pltpu.VMEM((2, BY, CZ), F32)]
         + [pltpu.VMEM((rows, CZ), BF16)] * 3
         + [pltpu.VMEM((2, HALF, BY, CPAD), F32)] * 2
         + [pltpu.VMEM((2, HALF, CY, CPAD), F32), pltpu.VMEM((2, KEPT, CY, CPAD), F32)]
+        + [pltpu.VMEM((5, CY, CZ), F32)] * 5
         + [tile, pltpu.VMEM((n1, 8, CZ), F32), tile, pltpu.VMEM((n2, 8, CZ), F32)]
         + [pltpu.SemaphoreType.DMA((8,)), pltpu.SemaphoreType.DMA((8,))]
         + [pltpu.SemaphoreType.DMA((3,))]

time: 80.3 us -> 66.4 us (0.83)
  Pallas kernels: 74.9 us -> 60.9 us
    pallas_call x1, Pallas kernels: 74.9 us -> 60.9 us  [per_device(): pl.pallas_call(functools.partial(kernel, sizes), out_shape=[jax.ShapeDtyp...]
where the time goes in v1:
time: 66.4 us; the launch traced here: 66.2 us
  Pallas kernels  60.9 us (92%)
  local copies, waits for them, and re-layouts  4.59 us (7%)
    pallas_call x1, Pallas kernels, per_device(): pl.pallas_call(functools.partial(kernel, sizes), out_shape=[jax.ShapeDtyp...  60.9 us
    unnamed x5, local copies, waits for them, and re-layouts  4.59 us

profile of v1, /device:TPU:0, one launch (start us, length us, event | category | flops | bytes accessed | tf_op | source)
XLA Modules:
  0.0 66.2 jit_solution(11402761337443323162)
XLA Ops:
  0.6 60.9 %shard_map.184 = (f32[32,32,128]{2,1,0:T(8,128)}, f32[32,32,128]{2,1,0:T(8,128)}, f32[32,32,128]{2,1,0:T(8,128)}) custom-call(f32[32,32,128]{2,1,0:T(8,128)} %refs_0_.1, f32[32,32,128]{2,1,0:T(8,128)} %refs_1_.1, f32[32,32,128]{2,1,0:T(8,128)} %refs_2_.1, f32[32,32,128]{2,1,0:T(8,128)} %refs_3_.1, f32[32,32,128]{2,1,0:T(8,128)} %refs_4_.1, ...), custom_call_target="tpu_custom_call" | custom-call | tf_op jit(solution)/shard_map/pallas_call | solution.py:625
  61.6 0.0 copy-start
  61.6 1.9 %copy.23 = f32[32,32,128]{2,1,0:T(8,128)} copy(f32[32,32,128]{2,1,0:T(8,128)} %get-tuple-element.6) | data formatting | bytes 1048576
  63.5 1.9 %copy.24 = f32[32,32,128]{2,1,0:T(8,128)} copy(f32[32,32,128]{2,1,0:T(8,128)} %get-tuple-element.7) | data formatting | bytes 1048576
  65.4 0.0 copy-done
  65.4 0.8 %copy.25 = f32[32,32,128]{2,1,0:T(8,128)} copy(f32[32,32,128]{2,1,0:T(8,128)S(1)} %copy-done) | data formatting | bytes 1048576
Async XLA Ops:
  61.6 3.8 %copy-start = (f32[32,32,128]{2,1,0:T(8,128)S(1)}, f32[32,32,128]{2,1,0:T(8,128)}, u32[]{:S(2)}) copy-start(f32[32,32,128]{2,1,0:T(8,128)} %get-tuple-element.8) | copy-start | bytes 1572868

commit v2 on v1

--- a/solution.py
+++ b/solution.py
@@ -89,7 +89,7 @@
     return both[:rows] + both[rows:] + mm(const[:rows], low)
 
 
-def sweep(body, init, count=CX, unroll=2):
+def sweep(body, init, count=CX, unroll=8):
     return lax.fori_loop(0, count, body, init, unroll=unroll)
 
 
@@ -339,10 +339,10 @@
                 source_ref, target_ref = rz_send.at[:, sy], rz.at[:, ty]
             far_copies.append(remote(source_ref, target_ref, device(dx, dy, 1)))
     for k in range(2):
-        lax.fori_loop(24 * k, 24 * k + 8, stage_r, 0, unroll=2)
+        lax.fori_loop(24 * k, 24 * k + 8, stage_r, 0, unroll=8)
         for copy in wide_copies[3 * k : 3 * k + 3]:
             copy.start()
-    lax.fori_loop(8, 24, stage_r, 0, unroll=2)
+    lax.fori_loop(8, 24, stage_r, 0, unroll=8)
     for copy in wide_copies[6:] + far_copies:
         copy.start()
     for copy in wide_copies + far_copies:
@@ -471,7 +471,7 @@
         image[x] = image[x] + at_faces(face_d, x)
         return carry
 
-    for send, recv, peers in ((ar_send1, ar_recv1, peers1), (ar_send2, ar_recv2, peers2)):
+    for send, recv, peers in ((ar_send1, ar_recv2, peers2), (ar_send2, ar_recv1, peers1)):
         copies = [remote(send, recv.at[i], peer) for i, peer in enumerate(peers)]
         for copy in copies:
             copy.start()
@@ -622,7 +622,7 @@
     )
     anywhere = pl.BlockSpec(memory_space=pl.ANY)
     in_specs = [anywhere] * 8 + [pl.BlockSpec(memory_space=pltpu.SMEM)] + [anywhere] * len(consts)
-    return pl.pallas_call(
+    results = pl.pallas_call(
         functools.partial(kernel, sizes),
         out_shape=[jax.ShapeDtypeStruct((CX, CY, CZ), F32)] * 3,
         in_specs=in_specs,
@@ -632,6 +632,19 @@
             collective_id=0, has_side_effects=True, vmem_limit_bytes=60 * 1024 * 1024
         ),
     )(*args, *(jnp.asarray(c) for c in consts))
+
+    whole = pl.BlockSpec((CX, CY, CZ), lambda: (0, 0, 0))
+    return pl.pallas_call(
+        handed_on,
+        out_shape=[jax.ShapeDtypeStruct((CX, CY, CZ), F32)] * 3,
+        in_specs=[whole] * 3,
+        out_specs=[whole] * 3,
+    )(*results)
+
+
+def handed_on(*refs):
+    for i in range(3):
+        refs[3 + i][...] = refs[i][...]
 
 
 def solution(mesh):

time: 66.4 us -> 56.6 us (0.85)
  Pallas kernels: 60.9 us -> 55.9 us
  local copies, waits for them, and re-layouts: 4.59 us -> 0 us
    pallas_call x1, Pallas kernels: 60.9 us -> 53.3 us  [per_device(): pl.pallas_call(functools.partial(kernel, sizes), out_shape=[jax.ShapeDtyp...]
    unnamed x5 -> x0, local copies, waits for them, and re-layouts: 4.59 us -> none
    pallas_call x0 -> x1, Pallas kernels: none -> 2.53 us  [per_device(): pl.pallas_call(handed_on, out_shape=[jax.ShapeDtypeStruct((CX, CY, CZ), F...]
where the time goes in v2:
time: 56.6 us; the launch traced here: 56.5 us
  Pallas kernels  55.9 us (99%)
  between operations  0.64 us (1%)
    pallas_call x1, Pallas kernels, per_device(): pl.pallas_call(functools.partial(kernel, sizes), out_shape=[jax.ShapeDtyp...  53.3 us
    pallas_call x1, Pallas kernels, per_device(): pl.pallas_call(handed_on, out_shape=[jax.ShapeDtypeStruct((CX, CY, CZ), F...  2.53 us

profile of v2, /device:TPU:0, one launch (start us, length us, event | category | flops | bytes accessed | tf_op | source)
XLA Modules:
  0.0 56.5 jit_solution(7103134206678946453)
XLA Ops:
  0.6 53.3 %shard_map.184 = (f32[32,32,128]{2,1,0:T(8,128)}, f32[32,32,128]{2,1,0:T(8,128)}, f32[32,32,128]{2,1,0:T(8,128)}) custom-call(f32[32,32,128]{2,1,0:T(8,128)} %refs_0_.1, f32[32,32,128]{2,1,0:T(8,128)} %refs_1_.1, f32[32,32,128]{2,1,0:T(8,128)} %refs_2_.1, f32[32,32,128]{2,1,0:T(8,128)} %refs_3_.1, f32[32,32,128]{2,1,0:T(8,128)} %refs_4_.1, ...), custom_call_target="tpu_custom_call" | custom-call | tf_op jit(solution)/shard_map/pallas_call | solution.py:625
  54.0 2.5 %shard_map.185 = (f32[32,32,128]{2,1,0:T(8,128)}, f32[32,32,128]{2,1,0:T(8,128)}, f32[32,32,128]{2,1,0:T(8,128)}) custom-call(f32[32,32,128]{2,1,0:T(8,128)} %get-tuple-element.6.refs_0_, f32[32,32,128]{2,1,0:T(8,128)} %get-tuple-element.7.refs_1_, f32[32,32,128]{2,1,0:T(8,128)} %get-tuple-element.8.refs_2_), custom_call_target="tpu_custom_call" | custom-call | tf_op jit(solution)/shard_map/pallas_call | solution.py:637

commit v3 on v2

--- a/solution.py
+++ b/solution.py
@@ -114,11 +114,19 @@
     mx, my, layer = lax.axis_index("gx"), lax.axis_index("gy"), lax.axis_index("gz")
 
     def device(dx, dy, dz):
-        return {
-            "gx": lax.rem(mx + n_gx + dx, n_gx),
-            "gy": lax.rem(my + n_gy + dy, n_gy),
-            "gz": lax.rem(layer + n_gz + dz, n_gz),
-        }
+        moved = {}
+        for axis, place, offset, size in (
+            ("gx", mx, dx, n_gx), ("gy", my, dy, n_gy), ("gz", layer, dz, n_gz)
+        ):
+            if offset % size:
+                moved[axis] = wrapped[axis, offset % size]
+        return moved
+
+    wrapped = {}
+    for axis, place, size in (("gx", mx, n_gx), ("gy", my, n_gy), ("gz", layer, n_gz)):
+        for offset in range(1, size):
+            there = place + offset
+            wrapped[axis, offset] = jnp.where(there >= size, there - size, there)
 
     peers1 = [device(dx, 0, dz) for dz in range(n_gz) for dx in range(n_gx) if dx or dz]
     peers2 = [device(0, dy, 0) for dy in range(1, n_gy)]
@@ -340,32 +348,47 @@
             far_copies.append(remote(source_ref, target_ref, device(dx, dy, 1)))
     for k in range(2):
         lax.fori_loop(24 * k, 24 * k + 8, stage_r, 0, unroll=8)
-        for copy in wide_copies[3 * k : 3 * k + 3]:
-            copy.start()
+        wide_copies[3 * k].start()
     lax.fori_loop(8, 24, stage_r, 0, unroll=8)
-    for copy in wide_copies[6:] + far_copies:
+    for copy in far_copies[6:7] + wide_copies[6:] + far_copies[:6] + far_copies[7:] + wide_copies[1:3] + wide_copies[4:6]:
         copy.start()
-    for copy in wide_copies + far_copies:
-        copy.wait()
-    for copy in const_loads:
-        copy.wait()
-
-    own_left = lax.broadcasted_iota(jnp.int32, (BY, CZ), 1) < CZ // 2
-    rz_all[0] = jnp.where(own_left, rxz[0], rz[0])
-    rz_all[1] = rz[1]
-    rz_all[2] = jnp.where(own_left, rz[2], rxz[1])
+    for copy in wide_copies:
+        copy.wait()
+
     wide_lane = lax.broadcasted_iota(jnp.int32, (BY, CZ), 1)
 
     def fold(i, carry):
         j = BX - 1 - i
         v, w = box[i], box[j]
-        hv = pltpu.roll(rz_all[i // 16], lax.rem(CZ - (i % 16) * 8, CZ), 1)
-        hw = pltpu.roll(rz_all[j // 16], lax.rem(CZ - (j % 16) * 8, CZ), 1)
-        for parity, (main, halo) in enumerate(((v + w, hv + hw), (v - w, hv - hw))):
+        for parity, main in enumerate((v + w, v - w)):
             rows = pl.ds(pl.multiple_of((parity * HALF + i) * BY, 16), BY)
             high, low = split(main)
             a_hi[rows, :] = high
             a_lo[rows, :] = low
+        return carry
+
+    sweep(fold, 0, HALF, 8)
+    for copy in const_loads:
+        copy.wait()
+    weights2 = wz2[layer]
+    for chunk in range(6):
+        rows = slice(chunk * 384, (chunk + 1) * 384)
+        high = a_hi[rows]
+        out = mm(jnp.concatenate([high, a_lo[rows]], axis=1), wz1[...]) + mm(high, weights2[:CZ])
+        z1[chunk // 3, (chunk % 3) * 8 : (chunk % 3) * 8 + 8] = out.reshape(8, BY, CPAD)
+    for copy in far_copies:
+        copy.wait()
+    own_left = wide_lane < CZ // 2
+    rz_all[0] = jnp.where(own_left, rxz[0], rz[0])
+    rz_all[1] = rz[1]
+    rz_all[2] = jnp.where(own_left, rz[2], rxz[1])
+
+    def fold_far(i, carry):
+        j = BX - 1 - i
+        hv = pltpu.roll(rz_all[i // 16], lax.rem(CZ - (i % 16) * 8, CZ), 1)
+        hw = pltpu.roll(rz_all[j // 16], lax.rem(CZ - (j % 16) * 8, CZ), 1)
+        for parity, halo in enumerate((hv + hw, hv - hw)):
+            rows = pl.ds(pl.multiple_of((parity * HALF + i) * BY, 16), BY)
             halo_high = halo.astype(BF16).astype(F32)
             halo_low = halo - halo_high
             tile = jnp.where(
@@ -378,15 +401,12 @@
             a_halo[rows, :] = tile.astype(BF16)
         return carry
 
-    sweep(fold, 0, HALF, 4)
-    weights2 = wz2[layer]
+    sweep(fold_far, 0, HALF, 24)
     for chunk in range(6):
         rows = slice(chunk * 384, (chunk + 1) * 384)
-        high = a_hi[rows]
-        out = mm(jnp.concatenate([high, a_lo[rows]], axis=1), wz1[...]) + mm(
-            jnp.concatenate([high, a_halo[rows]], axis=1), weights2
-        )
-        z1[chunk // 3, (chunk % 3) * 8 : (chunk % 3) * 8 + 8] = out.reshape(8, BY, CPAD)
+        planes = slice((chunk % 3) * 8, (chunk % 3) * 8 + 8)
+        out = mm(a_halo[rows], weights2[CZ:]).reshape(8, BY, CPAD)
+        z1[chunk // 3, planes] = z1[chunk // 3, planes] + out
     for parity in range(2):
         for block in range(BY // 8):
             rows = slice(block * 8, block * 8 + 8)
@@ -429,7 +449,7 @@
         put_rows(send3, 0, d, x)
         return along + d * box[x + W, W : W + CY, :], z_pack(pack_d, d, x)
 
-    along, pack_d = sweep(stage_c, (zero, zero))
+    along, pack_d = sweep(stage_c, (zero, zero), CX, 32)
     round3 = exchange(send3, recv3, (direc,), (pack_d,))
 
     def d_face(x):
@@ -471,12 +491,17 @@
         image[x] = image[x] + at_faces(face_d, x)
         return carry
 
+    def prepare(x, carry):
+        poro[x] = poro[x] / TIME_STEP
+        perm[x] = INJECT_RATE * wells[x].astype(F32)
+        outflow[x] = jnp.abs(fraction(sat[x], oil[x])[1])
+        return carry
+
     for send, recv, peers in ((ar_send1, ar_recv2, peers2), (ar_send2, ar_recv1, peers1)):
         copies = [remote(send, recv.at[i], peer) for i, peer in enumerate(peers)]
         for copy in copies:
             copy.start()
-        if send is ar_send1:
-            sweep(finish_image, 0)
+        sweep(finish_image if send is ar_send1 else prepare, 0)
         for copy in copies:
             copy.wait()
         result = send[...]
@@ -506,7 +531,7 @@
         flow_z = upwind(flux_z[x], f, pltpu.roll(f, CZ - 1, 1))
         balance = (fx_flow - flow_before) + (flow_high - flow_low)
         balance = balance + (flow_z - pltpu.roll(flow_z, 1, 1))
-        return balance - INJECT_RATE * wells[x].astype(F32)
+        return balance - perm[x]
 
     def inverse_of(storage, out_vals, sat_vals, oil_vals):
         _, slope = fraction(sat_vals, oil_vals)
@@ -526,10 +551,11 @@
         out_vals = out_vals + jnp.maximum(-flux_y[x, 7:39, :], 0.0)
         out_vals = out_vals + jnp.maximum(fz, 0.0) + jnp.maximum(-pltpu.roll(fz, 1, 1), 0.0)
         out_vals = out_vals + at_faces(face_o, x)
+        slope = outflow[x]
         outflow[x] = out_vals
         s = sat[x]
         balance = balance_of(frac0, flow, flow_before, x) + at_faces(face_f, x)
-        s_new = s - balance * inverse_of(poro[x] / TIME_STEP, out_vals, s, oil[x])
+        s_new = s - balance * (1.0 / (poro[x] + out_vals * slope))
         sat_b[x] = s_new
         f_new, _ = fraction(s_new, oil[x])
         frac1[x + 1, 8 : 8 + CY, :] = f_new
@@ -548,7 +574,7 @@
 
     def within(frac, x, flow_before):
         flow = upwind(flux_x[x + 1], mid(frac, x + 1), mid(frac, x + 2))
-        storage = poro[x] / TIME_STEP
+        storage = poro[x]
         s = sat_b[x]
         balance = balance_of(frac, flow, flow_before, x) + storage * (s - sat[x])
         inverse = inverse_of(storage, outflow[x], s, oil[x])
@@ -572,7 +598,7 @@
             copy.wait()
         for k in range(5):
             face_f[k] = upwind(face_p[k], send[k], recv[k])
-        return sweep(functools.partial(across, last), zero)
+        return sweep(functools.partial(across, last), zero, CX, 16)
 
     pack_f = later(frac1, send4, recv4, round4, False)
     round5 = exchange(send5, recv5, (frac2,), (pack_f,))

time: 56.6 us -> 54.3 us (0.959)
  Pallas kernels: 55.9 us -> 53.6 us
    pallas_call x1, Pallas kernels: 53.3 us -> 51 us  [per_device(): pl.pallas_call(functools.partial(kernel, sizes), out_shape=[jax.ShapeDtyp...]
where the time goes in v3:
time: 54.3 us; the launch traced here: 54.2 us
  Pallas kernels  53.6 us (99%)
  between operations  0.64 us (1%)
    pallas_call x1, Pallas kernels, per_device(): pl.pallas_call(functools.partial(kernel, sizes), out_shape=[jax.ShapeDtyp...  51 us
    pallas_call x1, Pallas kernels, per_device(): pl.pallas_call(handed_on, out_shape=[jax.ShapeDtypeStruct((CX, CY, CZ), F...  2.53 us

profile of v3, /device:TPU:0, one launch (start us, length us, event | category | flops | bytes accessed | tf_op | source)
XLA Modules:
  0.0 54.2 jit_solution(7850478294841425427)
XLA Ops:
  0.6 51.0 %shard_map.184 = (f32[32,32,128]{2,1,0:T(8,128)}, f32[32,32,128]{2,1,0:T(8,128)}, f32[32,32,128]{2,1,0:T(8,128)}) custom-call(f32[32,32,128]{2,1,0:T(8,128)} %refs_0_.1, f32[32,32,128]{2,1,0:T(8,128)} %refs_1_.1, f32[32,32,128]{2,1,0:T(8,128)} %refs_2_.1, f32[32,32,128]{2,1,0:T(8,128)} %refs_3_.1, f32[32,32,128]{2,1,0:T(8,128)} %refs_4_.1, ...), custom_call_target="tpu_custom_call" | custom-call | tf_op jit(solution)/shard_map/pallas_call | solution.py:651
  51.7 2.5 %shard_map.185 = (f32[32,32,128]{2,1,0:T(8,128)}, f32[32,32,128]{2,1,0:T(8,128)}, f32[32,32,128]{2,1,0:T(8,128)}) custom-call(f32[32,32,128]{2,1,0:T(8,128)} %get-tuple-element.6.refs_0_, f32[32,32,128]{2,1,0:T(8,128)} %get-tuple-element.7.refs_1_, f32[32,32,128]{2,1,0:T(8,128)} %get-tuple-element.8.refs_2_), custom_call_target="tpu_custom_call" | custom-call | tf_op jit(solution)/shard_map/pallas_call | solution.py:663

commit v4 on v3

--- a/solution.py
+++ b/solution.py
@@ -349,7 +349,7 @@
     for k in range(2):
         lax.fori_loop(24 * k, 24 * k + 8, stage_r, 0, unroll=8)
         wide_copies[3 * k].start()
-    lax.fori_loop(8, 24, stage_r, 0, unroll=8)
+    lax.fori_loop(8, 24, stage_r, 0, unroll=16)
     for copy in far_copies[6:7] + wide_copies[6:] + far_copies[:6] + far_copies[7:] + wide_copies[1:3] + wide_copies[4:6]:
         copy.start()
     for copy in wide_copies:
@@ -598,7 +598,7 @@
             copy.wait()
         for k in range(5):
             face_f[k] = upwind(face_p[k], send[k], recv[k])
-        return sweep(functools.partial(across, last), zero, CX, 16)
+        return sweep(functools.partial(across, last), zero, CX, 32)
 
     pack_f = later(frac1, send4, recv4, round4, False)
     round5 = exchange(send5, recv5, (frac2,), (pack_f,))

time: 54.3 us -> 54.7 us (level)
  no operation moved by 1% of the time
where the time goes in v4:
time: 54.7 us; the launch traced here: 54.5 us
  Pallas kernels  53.9 us (99%)
  between operations  0.64 us (1%)
    pallas_call x1, Pallas kernels, per_device(): pl.pallas_call(functools.partial(kernel, sizes), out_shape=[jax.ShapeDtyp...  51.4 us
    pallas_call x1, Pallas kernels, per_device(): pl.pallas_call(handed_on, out_shape=[jax.ShapeDtypeStruct((CX, CY, CZ), F...  2.53 us

profile of v4, /device:TPU:0, one launch (start us, length us, event | category | flops | bytes accessed | tf_op | source)
XLA Modules:
  0.0 54.5 jit_solution(9125842903321662081)
XLA Ops:
  0.6 51.4 %shard_map.184 = (f32[32,32,128]{2,1,0:T(8,128)}, f32[32,32,128]{2,1,0:T(8,128)}, f32[32,32,128]{2,1,0:T(8,128)}) custom-call(f32[32,32,128]{2,1,0:T(8,128)} %refs_0_.1, f32[32,32,128]{2,1,0:T(8,128)} %refs_1_.1, f32[32,32,128]{2,1,0:T(8,128)} %refs_2_.1, f32[32,32,128]{2,1,0:T(8,128)} %refs_3_.1, f32[32,32,128]{2,1,0:T(8,128)} %refs_4_.1, ...), custom_call_target="tpu_custom_call" | custom-call | tf_op jit(solution)/shard_map/pallas_call | solution.py:651
  52.0 2.5 %shard_map.185 = (f32[32,32,128]{2,1,0:T(8,128)}, f32[32,32,128]{2,1,0:T(8,128)}, f32[32,32,128]{2,1,0:T(8,128)}) custom-call(f32[32,32,128]{2,1,0:T(8,128)} %get-tuple-element.6.refs_0_, f32[32,32,128]{2,1,0:T(8,128)} %get-tuple-element.7.refs_1_, f32[32,32,128]{2,1,0:T(8,128)} %get-tuple-element.8.refs_2_), custom_call_target="tpu_custom_call" | custom-call | tf_op jit(solution)/shard_map/pallas_call | solution.py:663
